TPU v7x, 32 devices: a whole 2x2x4 slice. The times are simulated.
32 devices in a mesh: groups: 2 (over y), expert: 4 (over z), tensor: 4 (over x, core).
Axes of the slice: x: 2, y: 2, z: 4, core: 2. Of those that a mesh axis runs over, the one named last changes fastest.
Arguments:
- source_states: bfloat16 [2048, 2048], P(('groups', 'expert')), parts along dimension 0, may hold values from -6 to 6
- routes: int32 [2048, 2], P(('groups', 'expert')), parts along dimension 0, may hold values from 0 to 3, all different within a row; in each aligned block of 256 rows (0 to 255, 256 to 511, ...) at most 256 rows name the same one
- router_weight: bfloat16 [2048, 4], replicated, may hold values from -0.125 to 0.125
- fc1_weight: bfloat16 [4, 2048, 8192], P('expert', None, 'tensor'), may hold values from -0.125 to 0.125
- fc2_weight: bfloat16 [4, 8192, 2048], P('expert', 'tensor'), may hold values from -0.09375 to 0.09375
- lengths: int32 [8, 8], P(('groups', 'expert')), parts along dimension 0, may hold values from 1 to 48, 256 in all within a row
- lang_ids: int32 [64, 6], P(('groups', 'expert')), parts along dimension 0, may hold values from 0 to 5, each once within a row
- pivot_states: bfloat16 [6, 2048], replicated, may hold values from -480 to 480
- query_weight: bfloat16 [2048, 2048], P(None, 'tensor'), may hold values from -0.125 to 0.125
- key_weight: bfloat16 [2048, 2048], P(None, 'tensor'), may hold values from -0.125 to 0.125
- value_weight: bfloat16 [2048, 2048], P(None, 'tensor'), may hold values from -0.125 to 0.125
- out_weight: bfloat16 [2048, 2048], P('tensor'), may hold values from -0.125 to 0.125
Outputs:
- encoded_states: bfloat16 [2048, 2048], P(('groups', 'expert'), 'tensor'), parts along dimension 0
- decoder_states: bfloat16 [384, 2048], P(('groups', 'expert')), parts along dimension 0
There are 2 independent parts, one for each index of `groups`. A program takes and returns all parts, laid end to end along the dimension named above; an argument that names none is the same for every part. Nothing has to cross between parts.
Inputs may be any that keep to these rules, and one draw needn't show every extreme that they name: `routes`: each token names two different experts; among the 256 tokens of one block no expert is named more than 256 times. `lengths`: each row sums to 256. `lang_ids`: each row names every pivot language once.
All inputs are finite; a program needn't handle non-finite values.
Results may differ from a plain program's by a relative error of at most 0.012.
Values may be sent and summed in bfloat16 or wider, within the bound.
A program may use at most 128 MiB of HBM per device.

v0:
```python
import jax
import jax.numpy as jnp
from jax import lax
from jax.sharding import PartitionSpec as P

HD = 128


EPSILON = 1e-05
NEGATIVE = -1e30


def normalize(values):
    values = values.astype(jnp.float32)
    center = jnp.mean(values, axis=-1, keepdims=True)
    shifted = values - center
    spread = jnp.mean(shifted * shifted, axis=-1, keepdims=True)
    return shifted * lax.rsqrt(spread + EPSILON)


def route_tables(routes, experts, capacity):
    tok_count = routes.shape[0]
    expert_iota = jnp.arange(experts, dtype=jnp.int32)
    chosen = routes[:, :, None] == expert_iota[None, None, :]
    flat_chosen = chosen.reshape(tok_count * 2, experts).astype(jnp.int32)
    before = jnp.cumsum(flat_chosen, axis=0) - flat_chosen
    slots = jnp.sum(before * flat_chosen, axis=1).reshape(tok_count, 2)
    slot_iota = jnp.arange(capacity, dtype=jnp.int32)
    placed = chosen[:, :, :, None] & (slots[:, :, None, None] == slot_iota[None, None, None, :])
    return (chosen, placed.reshape(tok_count, 2, experts * capacity).astype(jnp.bfloat16))


def project_pair(key_weight, value_weight):

    def project(totals, shard_part, offset):
        return (
            jnp.dot(shard_part, key_weight, preferred_element_type=jnp.float32),
            jnp.dot(shard_part, value_weight, preferred_element_type=jnp.float32),
        )

    return project


def shards(
    source_states,
    routes,
    router_weight,
    fc1_weight,
    fc2_weight,
    lengths,
    lang_ids,
    pivot_states,
    query_weight,
    key_weight,
    value_weight,
    out_weight,
):
    tok_count, model_width = source_states.shape
    experts = router_weight.shape[1]
    capacity = 4 * tok_count // experts
    tensor_count = lax.axis_size("tensor")
    column_width = model_width // tensor_count
    column_start = lax.axis_index("tensor") * column_width
    normed = normalize(source_states).astype(jnp.bfloat16)
    logits = jnp.dot(normed, router_weight, preferred_element_type=jnp.float32)
    chosen, placed = route_tables(routes, experts, capacity)
    pair_logits = jnp.sum(jnp.where(chosen, logits[:, None, :], 0.0), axis=2)
    gate_values = jax.nn.sigmoid(pair_logits - pair_logits[:, ::-1])
    occupied = jnp.sum(placed, axis=1)
    outgoing = jnp.einsum("ts,td->sd", occupied, normed, preferred_element_type=jnp.float32)
    outgoing = outgoing.astype(jnp.bfloat16).reshape(experts, capacity, model_width)
    weight_in = fc1_weight[0]
    weight_back = fc2_weight[0]
    arrived = lax.all_to_all(outgoing, "expert", split_axis=0, concat_axis=0, tiled=True)
    row_block = arrived.reshape(-1, model_width)
    hidden = jnp.maximum(
        jnp.dot(row_block, weight_in, preferred_element_type=jnp.float32), 0.0
    ).astype(jnp.bfloat16)
    partial_value = jnp.dot(hidden, weight_back, preferred_element_type=jnp.float32).astype(
        jnp.bfloat16
    )
    partials = partial_value.reshape(arrived.shape)
    zeroed = jnp.zeros((tok_count, key_weight.shape[1]), jnp.float32)
    project = project_pair(key_weight, value_weight)
    own_cols = lax.dynamic_slice_in_dim(source_states, column_start, column_width, 1).astype(
        jnp.float32
    )
    widened = partials.astype(jnp.float32)
    summed = lax.psum_scatter(
        widened.astype(jnp.bfloat16), "tensor", scatter_dimension=2, tiled=True
    )
    returned_rows = lax.all_to_all(summed, "expert", split_axis=0, concat_axis=0, tiled=True)
    picked = jnp.einsum(
        "tks,sd->tkd",
        placed,
        returned_rows.reshape(experts * capacity, column_width),
        preferred_element_type=jnp.float32,
    )
    encoded = (own_cols + jnp.sum(gate_values[:, :, None] * picked, axis=1)).astype(jnp.bfloat16)
    key_sum, value_sum = project(
        (zeroed, zeroed), lax.all_gather(encoded, "tensor", axis=1, tiled=True), jnp.int32(0)
    )
    key_cache = key_sum.astype(jnp.bfloat16)
    value_cache = value_sum.astype(jnp.bfloat16)
    query_count = lengths.shape[1]
    pivot_count = pivot_states.shape[0]
    row_count = query_count * pivot_count
    query_ends = jnp.cumsum(lengths[0])
    positions = jnp.arange(tok_count, dtype=jnp.int32)
    key_owner = jnp.sum((positions[:, None] >= query_ends[None, :]).astype(jnp.int32), axis=1)
    row_owner = jnp.arange(row_count, dtype=jnp.int32) // pivot_count
    allowed = row_owner[:, None] == key_owner[None, :]
    language_pick = (
        lang_ids.reshape(-1)[:, None] == jnp.arange(pivot_count, dtype=jnp.int32)[None, :]
    ).astype(jnp.bfloat16)
    decoder_in = jnp.dot(language_pick, pivot_states, preferred_element_type=jnp.float32).astype(
        jnp.bfloat16
    )
    queries = jnp.dot(decoder_in, query_weight, preferred_element_type=jnp.float32).astype(
        jnp.bfloat16
    )
    head_local = queries.shape[1] // HD
    query_heads = queries.reshape(row_count, head_local, HD)
    key_heads = key_cache.reshape(tok_count, head_local, HD)
    value_heads = value_cache.reshape(tok_count, head_local, HD)
    scores = jnp.einsum(
        "rhe,the->hrt", query_heads, key_heads, preferred_element_type=jnp.float32
    ) * HD ** (-0.5)
    scores = jnp.where(allowed[None], scores, NEGATIVE)
    row_max = jnp.max(scores, axis=2, keepdims=True)
    weights = jnp.exp(scores - row_max)
    attention = (weights / jnp.sum(weights, axis=2, keepdims=True)).astype(jnp.bfloat16)
    context = jnp.einsum(
        "hrt,the->rhe", attention, value_heads, preferred_element_type=jnp.float32
    ).astype(jnp.bfloat16)
    partial_out = jnp.dot(
        context.reshape(row_count, head_local * HD), out_weight, preferred_element_type=jnp.float32
    )
    attn_total = lax.psum(partial_out.astype(jnp.bfloat16), "tensor").astype(jnp.float32)
    decoded = normalize(decoder_in.astype(jnp.float32) + attn_total).astype(jnp.bfloat16)
    return (encoded, decoded)


def solution(mesh):
    in_specs = (
        P(("groups", "expert"), None),
        P(("groups", "expert"), None),
        P(),
        P("expert", None, "tensor"),
        P("expert", "tensor", None),
        P(("groups", "expert"), None),
        P(("groups", "expert"), None),
        P(),
        P(None, "tensor"),
        P(None, "tensor"),
        P(None, "tensor"),
        P("tensor", None),
    )
    out_specs = (P(("groups", "expert"), "tensor"), P(("groups", "expert"), None))
    return jax.shard_map(shards, mesh=mesh, in_specs=in_specs, out_specs=out_specs, check_vma=False)
```

profile of v0, /device:TPU:1, one launch (start us, length us, event | category | flops | bytes accessed | tf_op | source)
XLA Modules:
  0.0 281.2 jit_solution(7772362713964266053)
XLA Ops:
  7.2 1.0 copy.39
  8.5 0.7 iota_compare_fusion.6
  9.2 1.2 reduce-window.18
  10.4 0.2 slice_reduce_fusion
  11.3 1.3 fusion.32
  12.7 2.1 copy.42
  14.7 0.2 convert_reduce_fusion
  15.0 0.4 fusion.14
  15.4 0.4 copy-done.2
  15.8 1.4 convolution_convert_fusion
  17.2 97.6 %all_to_all.10 = bf16[4,256,2048]{2,1,0:T(8,128)(2,1)} all-to-all(bf16[4,256,2048]{2,1,0:T(8,128)(2,1)S(1)} %bitcast.88), channel_id=1, replica_groups=mesh['groups'=2,'expert'=4,'tensor'=4] {'expert'}, dimensions={0} | all-to-all | bytes 8388608 | tf_op jit(solution)/shard_map/all_to_all | solution.py:74
  114.8 25.4 %fusion.7 = bf16[1024,2048]{1,0:T(8,128)(2,1)} fusion(bf16[1,2048,2048]{2,1,0:T(8,128)(2,1)} %param.16, bf16[1024,2048]{1,0:T(8,128)(2,1)} %bitcast.90, bf16[1,2048,2048]{2,1,0:T(8,128)(2,1)} %param.15), kind=kOutput, calls=%fused_computation.6 | convolution fusion | flops 17186160640 | bytes 25165824 | tf_op jit(solution)/shard_map/dot_general | solution.py:79
  140.2 45.2 %reduce-scatter.2.cloned.1.call-done = bf16[4,256,512]{2,1,0:T(8,128)(2,1)} async-done(((bf16[4,256,2048]{2,1,0:T(8,128)(2,1)}), bf16[4,256,512]{2,1,0:T(8,128)(2,1)}) %reduce-scatter.2.cloned.1.call-update) | async-done | bytes 1048592 | tf_op jit(solution)/shard_map/reduce_scatter | solution.py:89
  185.4 4.3 %all-to-all-start.1 = ((bf16[4,256,512]{2,1,0:T(8,128)(2,1)}), bf16[4,256,512]{2,1,0:T(8,128)(2,1)}, u32[]{:S(2)}, u32[]{:S(2)}) async-start(bf16[4,256,512]{2,1,0:T(8,128)(2,1)} %reduce-scatter.2.cloned.1.call-done), calls=%async_computation.2 | async-start | bytes 2097152 | tf_op jit(solution)/shard_map/all_to_all | solution.py:92
  189.7 0.4 fusion.54
  190.3 24.7 %all-to-all-done.1 = bf16[4,256,512]{2,1,0:T(8,128)(2,1)} async-done(((bf16[4,256,512]{2,1,0:T(8,128)(2,1)}), bf16[4,256,512]{2,1,0:T(8,128)(2,1)}, u32[]{:S(2)}, u32[]{:S(2)}) %all-to-all-start.1) | async-done | bytes 1048608 | tf_op jit(solution)/shard_map/all_to_all | solution.py:92
  215.0 2.3 fusion.22
  217.3 0.8 add_convert_fusion
  218.2 0.2 reduce-window.20
  218.6 0.2 convolution_convert_fusion.2
  218.9 2.1 fusion.31
  220.9 13.4 %all-gather.2.cloned.1.call-done = bf16[256,2048]{1,0:T(8,128)(2,1)} async-done(((bf16[256,512]{1,0:T(8,128)(2,1)}), bf16[256,2048]{1,0:T(8,128)(2,1)}) %all-gather.2.cloned.1.call-update) | async-done | bytes 1048592 | tf_op jit(solution)/shard_map/all_gather | solution.py:101
  234.3 2.1 fusion.27
  236.4 0.2 fusion.28
  236.6 0.2 fusion.56
  236.8 0.7 fusion.26
  237.5 0.4 fusion.30
  237.9 2.8 convolution_convert_fusion.1
  240.7 30.0 %all-reduce.2.cloned.1.call-done = bf16[48,2048]{1,0:T(8,128)(2,1)} async-done(((bf16[48,2048]{1,0:T(8,128)(2,1)}), bf16[48,2048]{1,0:T(8,128)(2,1)}) %all-reduce.2.cloned.1.call-update) | async-done | bytes 196624 | tf_op jit(solution)/shard_map/psum | solution.py:139
  270.7 1.1 fusion.37
  271.8 1.1 multiply_reduce_fusion
  273.0 1.7 multiply_convert_fusion
  (45 shorter events, 1.5 us)
Async XLA Ops:
  7.2 227.2 %copy-start = (bf16[2048,512]{1,0:T(8,128)(2,1)S(1)}, bf16[2048,512]{1,0:T(8,128)(2,1)}, u32[]{:S(2)}) copy-start(bf16[2048,512]{1,0:T(8,128)(2,1)} %param.21) | copy-start | bytes 6291460
  7.2 7.6 %copy-start.1 = (bf16[256,2048]{1,0:T(8,128)(2,1)S(1)}, bf16[256,2048]{1,0:T(8,128)(2,1)}, u32[]{:S(2)}) copy-start(bf16[256,2048]{1,0:T(8,128)(2,1)} %param.12) | copy-start | bytes 3145732
  7.2 178.2 %reduce-scatter.2.cloned.1.call-start = ((), (), s32[]{:S(2)}) async-start(), calls=%async_computation.3 | async-start | bytes 5242880 | tf_op jit(solution)/shard_map/reduce_scatter | solution.py:89
  14.7 1.0 copy-start.2
  140.2 49.5 %copy-start.8 = (bf16[2048,4]{0,1:T(4,128)(2,1)S(1)}, bf16[2048,4]{0,1:T(4,128)(2,1)}, u32[]{:S(2)}) copy-start(bf16[2048,4]{0,1:T(4,128)(2,1)} %param.14) | copy-start | bytes 49156
  140.2 49.9 %copy-start.4 = (s32[256,2]{0,1:T(2,128)S(1)}, s32[256,2]{0,1:T(2,128)}, u32[]{:S(2)}) copy-start(s32[256,2]{0,1:T(2,128)} %param.13) | copy-start | bytes 6148
  185.4 29.6 %all-to-all-start.1 = ((bf16[4,256,512]{2,1,0:T(8,128)(2,1)}), bf16[4,256,512]{2,1,0:T(8,128)(2,1)}, u32[]{:S(2)}, u32[]{:S(2)}) async-start(bf16[4,256,512]{2,1,0:T(8,128)(2,1)} %reduce-scatter.2.cloned.1.call-done), calls=%async_computation.2 | async-start | bytes 2097152 | tf_op jit(solution)/shard_map/all_to_all | solution.py:92
  189.7 44.6 %all-gather.2.cloned.1.call-start = ((), (), s32[]{:S(2)}) async-start(), calls=%async_computation.4 | async-start | bytes 1310720 | tf_op jit(solution)/shard_map/all_gather | solution.py:101
  190.3 27.9 %copy-start.5 = (s32[8,6]{1,0:T(8,128)S(1)}, s32[8,6]{1,0:T(8,128)}, u32[]{:S(2)}) copy-start(s32[8,6]{1,0:T(8,128)} %param.18) | copy-start | bytes 580
  190.3 28.0 %copy-start.9 = (s32[1,8]{1,0:T(1,128)S(1)}, s32[1,8]{1,0:T(1,128)}, u32[]{:S(2)}) copy-start(s32[1,8]{1,0:T(1,128)} %param.17) | copy-start | bytes 100
  190.3 28.3 %copy-start.3 = (bf16[6,2048]{1,0:T(8,128)(2,1)S(1)}, bf16[6,2048]{1,0:T(8,128)(2,1)}, u32[]{:S(2)}) copy-start(bf16[6,2048]{1,0:T(8,128)(2,1)} %param.19) | copy-start | bytes 73732
  218.1 52.6 %all-reduce.2.cloned.1.call-start = ((), (), s32[]{:S(2)}) async-start(), calls=%async_computation.5 | async-start | bytes 393216 | tf_op jit(solution)/shard_map/psum | solution.py:139
  234.3 2.5 copy-start.6
  234.3 2.5 copy-start.7
Sparse Core Ops, SparseCore 0:
  140.3 45.0 reduce-scatter.1
  218.2 16.0 all-gather.1
  240.8 29.8 all-reduce.1
where the time goes:
time: 284 us; the launch traced here: 281 us
  waiting for transfers between devices  113 us (40%)
  blocking collectives  97.6 us (34%)
  matrix products  37.9 us (13%)
  between operations  14 us (5%)
  other arithmetic  9.69 us (3%)
  starting transfers between devices  4.39 us (2%)
  local copies, waits for them, and re-layouts  4.36 us (2%)
    all_to_all x1, blocking collectives, shards(): lax.all_to_all(outgoing, 'expert', split_axis=0, concat_axis=0, tiled=True)  97.6 us
    reduce_scatter x1, waiting for transfers between devices, shards(): lax.psum_scatter(widened.astype(jnp.bfloat16), 'tensor', scatter_dimensio...  45.2 us
    psum x1, waiting for transfers between devices, shards(): lax.psum(partial_out.astype(jnp.bfloat16), 'tensor').astype(jnp.float32)  30 us
    dot_general x1, matrix products, shards(): jnp.dot(hidden, weight_back, preferred_element_type=jnp.float32)  25.4 us
    all_to_all x1, waiting for transfers between devices, shards(): lax.all_to_all(summed, 'expert', split_axis=0, concat_axis=0, tiled=True)  24.7 us
    all_gather x1, waiting for transfers between devices, shards(): lax.all_gather(encoded, 'tensor', axis=1, tiled=True)  13.4 us
  transfers between devices with their start and end apart: 4, of which 4 were waited for; matrix products, arithmetic and copies ran while one was open for 1% of the time, Pallas kernels for 0%

commit v1 on v0

--- a/solution.py
+++ b/solution.py
@@ -1,6 +1,10 @@
+import functools
+
 import jax
 import jax.numpy as jnp
 from jax import lax
+from jax.experimental import pallas as pl
+from jax.experimental.pallas import tpu as pltpu
 from jax.sharding import PartitionSpec as P
 
 HD = 128
@@ -22,9 +26,12 @@
     tok_count = routes.shape[0]
     expert_iota = jnp.arange(experts, dtype=jnp.int32)
     chosen = routes[:, :, None] == expert_iota[None, None, :]
-    flat_chosen = chosen.reshape(tok_count * 2, experts).astype(jnp.int32)
-    before = jnp.cumsum(flat_chosen, axis=0) - flat_chosen
-    slots = jnp.sum(before * flat_chosen, axis=1).reshape(tok_count, 2)
+    flat_chosen = chosen.reshape(tok_count * 2, experts).astype(jnp.bfloat16)
+    pair_iota = jnp.arange(tok_count * 2, dtype=jnp.int32)
+    earlier = (pair_iota[None, :] < pair_iota[:, None]).astype(jnp.bfloat16)
+    before = jnp.dot(earlier, flat_chosen, preferred_element_type=jnp.float32)
+    slots = jnp.sum(before * flat_chosen.astype(jnp.float32), axis=1)
+    slots = slots.astype(jnp.int32).reshape(tok_count, 2)
     slot_iota = jnp.arange(capacity, dtype=jnp.int32)
     placed = chosen[:, :, :, None] & (slots[:, :, None, None] == slot_iota[None, None, None, :])
     return (chosen, placed.reshape(tok_count, 2, experts * capacity).astype(jnp.bfloat16))
@@ -41,7 +48,7 @@
     return project
 
 
-def shards(
+def packed_shards(
     source_states,
     routes,
     router_weight,
@@ -105,7 +112,10 @@
     query_count = lengths.shape[1]
     pivot_count = pivot_states.shape[0]
     row_count = query_count * pivot_count
-    query_ends = jnp.cumsum(lengths[0])
+    query_iota = jnp.arange(query_count, dtype=jnp.int32)
+    query_ends = jnp.sum(
+        jnp.where(query_iota[None, :] <= query_iota[:, None], lengths[0][None, :], 0), axis=1
+    )
     positions = jnp.arange(tok_count, dtype=jnp.int32)
     key_owner = jnp.sum((positions[:, None] >= query_ends[None, :]).astype(jnp.int32), axis=1)
     row_owner = jnp.arange(row_count, dtype=jnp.int32) // pivot_count
@@ -141,6 +151,521 @@
     return (encoded, decoded)
 
 
+MESH = pl.DeviceIdType.MESH
+TILE = 256
+
+
+def layer_kernel(
+    experts,
+    chips,
+    normed,
+    own_cols,
+    gates,
+    decoder_in,
+    queries,
+    mask,
+    fc1_hbm,
+    fc2_hbm,
+    key_hbm,
+    value_hbm,
+    out_hbm,
+    encoded,
+    decoded,
+    fc1,
+    fc2,
+    key_w,
+    value_w,
+    out_w,
+    rows,
+    hidden,
+    core_out,
+    core_in,
+    kept,
+    chip_out,
+    chip_in,
+    back_out,
+    back_in,
+    gathered,
+    key_sum,
+    value_sum,
+    context,
+    out_sum,
+    half_out,
+    half_in,
+    sum_out,
+    sum_in,
+    full_in,
+    load_sem,
+    own_sem,
+    up_sem,
+    down_sem,
+    line_recv,
+    send_sem,
+    recv_sem,
+    ret_send,
+    ret_recv,
+    gat_send,
+    gat_recv,
+    end_send,
+    end_recv,
+):
+    tokens, width = normed.shape
+    columns = own_cols.shape[1]
+    e = lax.axis_index("expert")
+    t = lax.axis_index("tensor")
+    chip, core = t // 2, t % 2
+    mate = chip * 2 + 1 - core
+    far = (1 - chip) * 2 + core
+    far_mate = (1 - chip) * 2 + 1 - core
+    tensor_peer = {"mate": {"tensor": mate}, "far": {"tensor": far}}
+
+    def same(i):
+        return 1 - ((e - i + experts) % experts + experts - 1) // experts
+
+    nearest = [sorted(range(experts), key=lambda b, i=i: abs(b - i)) for i in range(experts)]
+    order = [sum(same(i) * nearest[i][s] for i in range(experts)) for s in range(experts)]
+
+    loads = [
+        pltpu.make_async_copy(src, dst, load_sem.at[i])
+        for i, (src, dst) in enumerate(
+            ((fc1_hbm, fc1), (fc2_hbm, fc2), (key_hbm, key_w), (value_hbm, value_w), (out_hbm, out_w))
+        )
+    ]
+    for load in loads:
+        load.start()
+
+    barrier = pltpu.get_barrier_semaphore()
+    for step in range(1, experts):
+        pl.semaphore_signal(
+            barrier, 1, device_id={"expert": (e + step) % experts}, device_id_type=MESH
+        )
+    for peer in tensor_peer.values():
+        pl.semaphore_signal(barrier, 1, device_id=peer, device_id_type=MESH)
+
+    def quarter(q):
+        return pl.ds(pl.multiple_of(q * columns, columns), columns)
+
+    pl.semaphore_wait(barrier, experts + 1)
+
+    def line(b, up, from_own):
+        src = normed.at[:, quarter(t)] if from_own else rows.at[b, :, quarter(t)]
+        return pltpu.make_async_remote_copy(
+            src_ref=src,
+            dst_ref=rows.at[b, :, quarter(t)],
+            send_sem=(up_sem if up else down_sem).at[b],
+            recv_sem=line_recv.at[b],
+            device_id={"expert": (e + 1) % experts if up else (e + experts - 1) % experts},
+            device_id_type=MESH,
+        )
+
+    def spread(b, q, kind, peer):
+        return pltpu.make_async_remote_copy(
+            src_ref=rows.at[b, :, quarter(q)],
+            dst_ref=rows.at[b, :, quarter(q)],
+            send_sem=send_sem.at[kind, b],
+            recv_sem=recv_sem.at[kind, b],
+            device_id=tensor_peer[peer],
+            device_id_type=MESH,
+        )
+
+    @pl.when(e + 1 < experts)
+    def _():
+        line(e, True, True).start()
+
+    @pl.when(e > 0)
+    def _():
+        line(e, False, True).start()
+
+    def own_copy():
+        return pltpu.make_async_copy(normed, rows.at[e], own_sem)
+
+    own_copy().start()
+
+    def arrive(s):
+        b = order[s]
+        line(b, True, False).wait_recv()
+
+        @pl.when((b < e) & (e + 1 < experts))
+        def _():
+            line(b, True, False).start()
+
+        @pl.when((b > e) & (e > 0))
+        def _():
+            line(b, False, False).start()
+
+        spread(b, t, 0, "far").start()
+        spread(b, t, 1, "mate").start()
+
+    def relay(s):
+        b = order[s]
+        spread(b, far, 0, "far").wait_recv()
+        spread(b, far, 2, "mate").start()
+
+    def ready(s):
+        b = order[s]
+        spread(b, mate, 1, "mate").wait_recv()
+        spread(b, far_mate, 2, "mate").wait_recv()
+
+    def first(s):
+        b = order[s]
+
+        @pl.loop(0, hidden.shape[1] // TILE)
+        def _(j):
+            at = pl.ds(pl.multiple_of(j * TILE, TILE), TILE)
+            tile = jnp.dot(rows[b], fc1[:, at], preferred_element_type=jnp.float32)
+            hidden[:, at] = jnp.maximum(tile, 0.0).astype(jnp.bfloat16)
+
+    per = columns // TILE
+
+    def second(s):
+        @pl.loop(0, chips * per)
+        def _(j):
+            p, k = j // per, j % per
+            start = (p * 2 + 1 - core) * columns + k * TILE
+            at = pl.ds(pl.multiple_of(start, TILE), TILE)
+            tile = jnp.dot(hidden[...], fc2[:, at], preferred_element_type=jnp.float32)
+            core_out[s, p, :, pl.ds(pl.multiple_of(k * TILE, TILE), TILE)] = tile.astype(
+                jnp.bfloat16
+            )
+
+        pair_copy(s).start()
+
+        @pl.loop(0, chips * per)
+        def _(j):
+            p, k = j // per, j % per
+            start = (p * 2 + core) * columns + k * TILE
+            at = pl.ds(pl.multiple_of(start, TILE), TILE)
+            tile = jnp.dot(hidden[...], fc2[:, at], preferred_element_type=jnp.float32)
+            kept[s, p, :, pl.ds(pl.multiple_of(k * TILE, TILE), TILE)] = tile
+
+    def pair_copy(s):
+        return pltpu.make_async_remote_copy(
+            src_ref=core_out.at[s],
+            dst_ref=core_in.at[s],
+            send_sem=ret_send.at[0, s],
+            recv_sem=ret_recv.at[0, s],
+            device_id=tensor_peer["mate"],
+            device_id_type=MESH,
+        )
+
+    def chip_copy(s):
+        return pltpu.make_async_remote_copy(
+            src_ref=chip_out.at[s],
+            dst_ref=chip_in.at[s],
+            send_sem=ret_send.at[1, s],
+            recv_sem=ret_recv.at[1, s],
+            device_id=tensor_peer["far"],
+            device_id_type=MESH,
+        )
+
+    def back_copy(s, b):
+        return pltpu.make_async_remote_copy(
+            src_ref=back_out.at[s],
+            dst_ref=back_in.at[e],
+            send_sem=ret_send.at[2, s],
+            recv_sem=ret_recv.at[2, e],
+            device_id={"expert": b},
+            device_id_type=MESH,
+        )
+
+    def back_wait(i):
+        return pltpu.make_async_remote_copy(
+            src_ref=back_out.at[0],
+            dst_ref=back_in.at[i],
+            send_sem=ret_send.at[2, 0],
+            recv_sem=ret_recv.at[2, i],
+            device_id={"expert": i},
+            device_id_type=MESH,
+        )
+
+    def reduce_pair(s):
+        pair_copy(s).wait_recv()
+        other = 1 - chip
+        chip_out[s] = (kept[s, other] + core_in[s, other].astype(jnp.float32)).astype(jnp.bfloat16)
+        chip_copy(s).start()
+
+    def reduce_chips(s):
+        chip_copy(s).wait_recv()
+        total = (
+            kept[s, chip]
+            + core_in[s, chip].astype(jnp.float32)
+            + chip_in[s].astype(jnp.float32)
+        ).astype(jnp.bfloat16)
+        if s == 0:
+            back_in[e] = total
+        else:
+            back_out[s] = total
+            back_copy(s, order[s]).start()
+
+    own_copy().wait()
+    loads[0].wait()
+    first(0)
+    arrive(1)
+    loads[1].wait()
+    second(0)
+    arrive(2)
+    relay(1)
+    reduce_pair(0)
+    ready(1)
+    first(1)
+    arrive(3)
+    relay(2)
+    second(1)
+    reduce_chips(0)
+    reduce_pair(1)
+    relay(3)
+    ready(2)
+    first(2)
+    second(2)
+    reduce_chips(1)
+    reduce_pair(2)
+    ready(3)
+    first(3)
+    reduce_chips(2)
+    second(3)
+    reduce_pair(3)
+    reduce_chips(3)
+
+    for s in range(1, experts):
+        back_wait(order[s]).wait_recv()
+    mixed = own_cols[...].astype(jnp.float32)
+    for i in range(experts):
+        mixed = mixed + gates[:, i : i + 1] * back_in[i].astype(jnp.float32)
+    mixed = mixed.astype(jnp.bfloat16)
+    encoded[...] = mixed
+    gathered[:, quarter(t)] = mixed
+
+    def gather(q, kind, peer):
+        return pltpu.make_async_remote_copy(
+            src_ref=gathered.at[:, quarter(q)],
+            dst_ref=gathered.at[:, quarter(q)],
+            send_sem=gat_send.at[kind],
+            recv_sem=gat_recv.at[kind],
+            device_id=tensor_peer[peer],
+            device_id_type=MESH,
+        )
+
+    gather(t, 0, "far").start()
+    gather(t, 1, "mate").start()
+    for load in loads[2:]:
+        load.wait()
+
+    def project(q, fresh):
+        part = gathered[:, quarter(q)]
+        for weight, total in ((key_w, key_sum), (value_w, value_sum)):
+            term = jnp.dot(part, weight[quarter(q), :], preferred_element_type=jnp.float32)
+            total[...] = term if fresh else total[...] + term
+
+    project(t, True)
+    gather(mate, 1, "mate").wait_recv()
+    project(mate, False)
+    gather(far, 0, "far").wait_recv()
+    gather(far, 2, "mate").start()
+    project(far, False)
+    gather(far_mate, 2, "mate").wait_recv()
+    project(far_mate, False)
+
+    for h in range(columns // HD):
+        at = slice(h * HD, (h + 1) * HD)
+        scores = lax.dot_general(
+            queries[:, at],
+            key_sum[:, at].astype(jnp.bfloat16),
+            (((1,), (1,)), ((), ())),
+            preferred_element_type=jnp.float32,
+        ) * HD ** (-0.5)
+        scores = jnp.where(mask[...] > 0.5, scores, NEGATIVE)
+        weights = jnp.exp(scores - jnp.max(scores, axis=1, keepdims=True))
+        attention = (weights / jnp.sum(weights, axis=1, keepdims=True)).astype(jnp.bfloat16)
+        context[:, at] = jnp.dot(
+            attention, value_sum[:, at].astype(jnp.bfloat16), preferred_element_type=jnp.float32
+        ).astype(jnp.bfloat16)
+
+    half = width // 2
+
+    def side(c):
+        return pl.ds(pl.multiple_of(c * half, half), half)
+
+    out_sum[...] = jnp.dot(context[...], out_w[...], preferred_element_type=jnp.float32)
+    half_out[...] = out_sum[:, side(1 - core)].astype(jnp.bfloat16)
+
+    def end_copy(src, dst, kind, peer):
+        return pltpu.make_async_remote_copy(
+            src_ref=src,
+            dst_ref=dst,
+            send_sem=end_send.at[kind],
+            recv_sem=end_recv.at[kind],
+            device_id=tensor_peer[peer],
+            device_id_type=MESH,
+        )
+
+    ends = (
+        end_copy(half_out, half_in, 0, "mate"),
+        end_copy(sum_out, sum_in, 1, "far"),
+        end_copy(full_in.at[core], full_in.at[core], 2, "mate"),
+    )
+    ends[0].start()
+    ends[0].wait_recv()
+    pair_sum = out_sum[:, side(core)] + half_in[...].astype(jnp.float32)
+    sum_out[...] = pair_sum.astype(jnp.bfloat16)
+    ends[1].start()
+    ends[1].wait_recv()
+    full_in[core] = (pair_sum + sum_in[...].astype(jnp.float32)).astype(jnp.bfloat16)
+    ends[2].start()
+    end_copy(full_in.at[core], full_in.at[1 - core], 2, "mate").wait_recv()
+    total = jnp.concatenate([full_in[0], full_in[1]], axis=1).astype(jnp.float32)
+    decoded[...] = normalize(decoder_in[...].astype(jnp.float32) + total).astype(jnp.bfloat16)
+
+    @pl.when(e + 1 < experts)
+    def _():
+        line(e, True, True).wait_send()
+
+    @pl.when(e > 0)
+    def _():
+        line(e, False, True).wait_send()
+
+    for s in range(experts):
+        b = order[s]
+        if s > 0:
+
+            @pl.when((b < e) & (e + 1 < experts))
+            def _():
+                line(b, True, False).wait_send()
+
+            @pl.when((b > e) & (e > 0))
+            def _():
+                line(b, False, False).wait_send()
+
+            spread(b, t, 0, "far").wait_send()
+            spread(b, t, 1, "mate").wait_send()
+            spread(b, far, 2, "mate").wait_send()
+            back_copy(s, b).wait_send()
+        pair_copy(s).wait_send()
+        chip_copy(s).wait_send()
+    gather(t, 0, "far").wait_send()
+    gather(t, 1, "mate").wait_send()
+    gather(far, 2, "mate").wait_send()
+    for end in ends:
+        end.wait_send()
+
+
+def dense_shards(
+    source_states,
+    routes,
+    router_weight,
+    fc1_weight,
+    fc2_weight,
+    lengths,
+    lang_ids,
+    pivot_states,
+    query_weight,
+    key_weight,
+    value_weight,
+    out_weight,
+):
+    tok_count, model_width = source_states.shape
+    experts = router_weight.shape[1]
+    tensor_count = lax.axis_size("tensor")
+    chips = tensor_count // 2
+    columns = model_width // tensor_count
+    normed = normalize(source_states).astype(jnp.bfloat16)
+    logits = jnp.dot(normed, router_weight, preferred_element_type=jnp.float32)
+    chosen = routes[:, :, None] == jnp.arange(experts, dtype=jnp.int32)[None, None, :]
+    pair_logits = jnp.sum(jnp.where(chosen, logits[:, None, :], 0.0), axis=2)
+    gate_values = jax.nn.sigmoid(pair_logits - pair_logits[:, ::-1])
+    gates = jnp.sum(jnp.where(chosen, gate_values[:, :, None], 0.0), axis=1)
+    own_cols = lax.dynamic_slice_in_dim(
+        source_states, lax.axis_index("tensor") * columns, columns, 1
+    )
+    query_count = lengths.shape[1]
+    pivot_count = pivot_states.shape[0]
+    row_count = query_count * pivot_count
+    query_iota = jnp.arange(query_count, dtype=jnp.int32)
+    query_ends = jnp.sum(
+        jnp.where(query_iota[None, :] <= query_iota[:, None], lengths[0][None, :], 0), axis=1
+    )
+    positions = jnp.arange(tok_count, dtype=jnp.int32)
+    key_owner = jnp.sum((positions[:, None] >= query_ends[None, :]).astype(jnp.int32), axis=1)
+    row_owner = jnp.arange(row_count, dtype=jnp.int32) // pivot_count
+    mask = (row_owner[:, None] == key_owner[None, :]).astype(jnp.float32)
+    language_pick = (
+        lang_ids.reshape(-1)[:, None] == jnp.arange(pivot_count, dtype=jnp.int32)[None, :]
+    ).astype(jnp.bfloat16)
+    decoder_in = jnp.dot(language_pick, pivot_states, preferred_element_type=jnp.float32).astype(
+        jnp.bfloat16
+    )
+    queries = jnp.dot(decoder_in, query_weight, preferred_element_type=jnp.float32).astype(
+        jnp.bfloat16
+    )
+    vmem = pl.BlockSpec(memory_space=pltpu.VMEM)
+    hbm = pl.BlockSpec(memory_space=pl.ANY)
+    bf16, f32, dma = jnp.bfloat16, jnp.float32, pltpu.SemaphoreType.DMA
+    units = fc1_weight.shape[2]
+    half = model_width // 2
+    return pl.pallas_call(
+        functools.partial(layer_kernel, experts, chips),
+        out_shape=(
+            jax.ShapeDtypeStruct((tok_count, columns), bf16),
+            jax.ShapeDtypeStruct((row_count, model_width), bf16),
+        ),
+        in_specs=[vmem] * 6 + [hbm] * 5,
+        out_specs=(vmem, vmem),
+        scratch_shapes=[
+            pltpu.VMEM((model_width, units), bf16),
+            pltpu.VMEM((units, model_width), bf16),
+            pltpu.VMEM((model_width, columns), bf16),
+            pltpu.VMEM((model_width, columns), bf16),
+            pltpu.VMEM((columns, model_width), bf16),
+            pltpu.VMEM((experts, tok_count, model_width), bf16),
+            pltpu.VMEM((tok_count, units), bf16),
+            pltpu.VMEM((experts, chips, tok_count, columns), bf16),
+            pltpu.VMEM((experts, chips, tok_count, columns), bf16),
+            pltpu.VMEM((experts, chips, tok_count, columns), f32),
+            pltpu.VMEM((experts, tok_count, columns), bf16),
+            pltpu.VMEM((experts, tok_count, columns), bf16),
+            pltpu.VMEM((experts, tok_count, columns), bf16),
+            pltpu.VMEM((experts, tok_count, columns), bf16),
+            pltpu.VMEM((tok_count, model_width), bf16),
+            pltpu.VMEM((tok_count, columns), f32),
+            pltpu.VMEM((tok_count, columns), f32),
+            pltpu.VMEM((row_count, columns), bf16),
+            pltpu.VMEM((row_count, model_width), f32),
+            pltpu.VMEM((row_count, half), bf16),
+            pltpu.VMEM((row_count, half), bf16),
+            pltpu.VMEM((row_count, half), bf16),
+            pltpu.VMEM((row_count, half), bf16),
+            pltpu.VMEM((2, row_count, half), bf16),
+            dma((5,)),
+            dma,
+            dma((experts,)),
+            dma((experts,)),
+            dma((experts,)),
+            dma((3, experts)),
+            dma((3, experts)),
+            dma((3, experts)),
+            dma((3, experts)),
+            dma((3,)),
+            dma((3,)),
+            dma((3,)),
+            dma((3,)),
+        ],
+        compiler_params=pltpu.CompilerParams(
+            collective_id=0, has_side_effects=True, vmem_limit_bytes=60 * 2**20
+        ),
+    )(
+        normed,
+        own_cols,
+        gates,
+        decoder_in,
+        queries,
+        mask,
+        fc1_weight[0],
+        fc2_weight[0],
+        key_weight,
+        value_weight,
+        out_weight,
+    )
+
+
 def solution(mesh):
     in_specs = (
         P(("groups", "expert"), None),
@@ -157,4 +682,6 @@
         P("tensor", None),
     )
     out_specs = (P(("groups", "expert"), "tensor"), P(("groups", "expert"), None))
+    sizes = dict(mesh.shape)
+    shards = dense_shards if sizes["expert"] == 4 and sizes["tensor"] == 4 else packed_shards
     return jax.shard_map(shards, mesh=mesh, in_specs=in_specs, out_specs=out_specs, check_vma=False)

time: 284 us -> 109 us (0.38)
  waiting for transfers between devices: 113 us -> 0 us
  blocking collectives: 97.6 us -> 0 us
  Pallas kernels: 0 us -> 95.3 us
  matrix products: 37.9 us -> 1.71 us
  between operations: 14 us -> 0.77 us
  other arithmetic: 9.69 us -> 5.29 us
  starting transfers between devices: 4.39 us -> 0 us
    all_to_all x1 -> x0, blocking collectives: 97.6 us -> none  [shards(): lax.all_to_all(outgoing, 'expert', split_axis=0, concat_axis=0, tiled=True)]
    pallas_call x0 -> x1, Pallas kernels: none -> 95.3 us  [dense_shards(): pl.pallas_call(functools.partial(layer_kernel, experts, chips), out_shape...]
    reduce_scatter x1 -> x0, waiting for transfers between devices: 45.2 us -> none  [shards(): lax.psum_scatter(widened.astype(jnp.bfloat16), 'tensor', scatter_dimensio...]
    dot_general x11 -> x3, matrix products: 37.9 us -> 1.71 us  [the longest x1 1.09 us: dense_shards(): jnp.dot(decoder_in, query_weight, preferred_element_type=jnp.float32)]
    psum x1 -> x0, waiting for transfers between devices: 30 us -> none  [shards(): lax.psum(partial_out.astype(jnp.bfloat16), 'tensor').astype(jnp.float32)]
    all_to_all x1 -> x0, waiting for transfers between devices: 24.7 us -> none  [shards(): lax.all_to_all(summed, 'expert', split_axis=0, concat_axis=0, tiled=True)]
    all_gather x1 -> x0, waiting for transfers between devices: 13.4 us -> none  [shards(): lax.all_gather(encoded, 'tensor', axis=1, tiled=True)]
    all_to_all x1 -> x0, starting transfers between devices: 4.31 us -> none  [shards(): lax.all_to_all(summed, 'expert', split_axis=0, concat_axis=0, tiled=True)]
  transfers between devices with their start and end apart: 4 -> 0, of which waited for: 4 -> 0; matrix products, arithmetic and copies ran while one was open for 1% -> 0% of each run, Pallas kernels for 0% -> 0%
where the time goes in v1:
time: 109 us
  Pallas kernels  95.3 us (87%)
  local copies, waits for them, and re-layouts  5.69 us (5%)
  other arithmetic  5.29 us (5%)
  matrix products  1.71 us (2%)
    pallas_call x1, Pallas kernels, dense_shards(): pl.pallas_call(functools.partial(layer_kernel, experts, chips), out_shape...  95.3 us
    unnamed x16, local copies, waits for them, and re-layouts  3.32 us

profile of v1, /device:TPU:1, one launch (start us, length us, event | category | flops | bytes accessed | tf_op | source)
XLA Modules:
  0.0 108.8 jit_solution(5888374169315763362)
XLA Ops:
  0.6 0.0 copy-start
  0.6 0.0 copy-start.4
  0.7 0.9 select_reduce_fusion.2
  1.6 0.1 convert_reduce_fusion.1
  1.7 0.8 eq.44
  2.4 1.4 %convert_reduce_fusion = f32[256]{0:T(256)S(1)} fusion(bf16[256,2048]{1,0:T(8,128)(2,1)} %param.12), kind=kLoop, calls=%fused_computation.1 | loop fusion | flops 1048320 | bytes 1049600 | tf_op jit(solution)/shard_map/reduce_sum | solution.py:19
  3.9 0.0 copy-start.1
  3.9 1.7 %fusion.2 = f32[256]{0:T(256)S(1)} fusion(bf16[256,2048]{1,0:T(8,128)(2,1)} %param.12, f32[256]{0:T(256)S(1)} %broadcast_multiply_fusion), kind=kLoop, calls=%fused_computation.5 | loop fusion | flops 2096896 | bytes 1050624 | tf_op jit(solution)/shard_map/reduce_sum | solution.py:21
  5.6 0.7 compare_convert_fusion.mask
  6.3 0.0 copy-done.4
  6.4 0.2 convolution_convert_fusion.decoder_in
  6.6 0.0 copy-done
  6.6 0.0 copy-start.3
  6.6 0.0 copy-start.5
  6.6 1.1 convolution_convert_fusion.1.queries
  7.7 0.0 copy-done.1
  7.7 0.0 copy-start.6
  7.7 0.7 constant_dynamic-slice_fusion.own_cols
  8.5 0.3 fusion.3.normed
  8.8 0.0 copy-done.3
  8.8 0.0 copy-done.5
  8.8 0.0 copy-start.2
  8.8 0.4 fusion.5
  9.2 0.0 copy-done.6
  9.2 0.1 rev.3
  9.4 0.8 copy.16.gates
  10.2 0.0 copy-done.2
  10.2 95.3 %shard_map.131 = (bf16[256,512]{1,0:T(8,128)(2,1)}, bf16[48,2048]{1,0:T(8,128)(2,1)}) custom-call(bf16[256,2048]{1,0:T(8,128)(2,1)} %copy-done.2, bf16[256,512]{1,0:T(8,128)(2,1)} %constant_dynamic-slice_fusion.own_cols, f32[256,4]{1,0:T(8,128)} %copy.16.gates, bf16[48,2048]{1,0:T(8,128)(2,1)} %copy-done.3, ...), custom_call_target="tpu_custom_call" | custom-call | tf_op jit(solution)/shard_map/pallas_call | solution.py:604
  105.5 1.7 %copy.19 = bf16[256,512]{1,0:T(8,128)(2,1)} copy(bf16[256,512]{1,0:T(8,128)(2,1)} %get-tuple-element.4) | data formatting | bytes 524288
  107.1 1.6 %copy.20 = bf16[48,2048]{1,0:T(8,128)(2,1)} copy(bf16[48,2048]{1,0:T(8,128)(2,1)} %get-tuple-element.5) | data formatting | bytes 393216
  (6 shorter events, 0.1 us)
Async XLA Ops:
  0.6 6.0 %copy-start = (bf16[2048,512]{1,0:T(8,128)(2,1)S(1)}, bf16[2048,512]{1,0:T(8,128)(2,1)}, u32[]{:S(2)}) copy-start(bf16[2048,512]{1,0:T(8,128)(2,1)} %param.20) | copy-start | bytes 6291460
  0.6 5.7 %copy-start.4 = (bf16[6,2048]{1,0:T(8,128)(2,1)S(1)}, bf16[6,2048]{1,0:T(8,128)(2,1)}, u32[]{:S(2)}) copy-start(bf16[6,2048]{1,0:T(8,128)(2,1)} %param.19) | copy-start | bytes 73732
  3.9 3.8 %copy-start.1 = (bf16[256,2048]{1,0:T(8,128)(2,1)S(1)}, bf16[256,2048]{1,0:T(8,128)(2,1)}, u32[]{:S(2)}) copy-start(bf16[256,2048]{1,0:T(8,128)(2,1)} %param.12) | copy-start | bytes 3145732
  6.6 2.2 %copy-start.3 = (bf16[48,2048]{1,0:T(8,128)(2,1)}, bf16[48,2048]{1,0:T(8,128)(2,1)S(1)}, u32[]{:S(2)}) copy-start(bf16[48,2048]{1,0:T(8,128)(2,1)S(1)} %convolution_convert_fusion.decoder_in) | copy-start | bytes 589828
  6.6 2.2 %copy-start.5 = (bf16[2048,4]{0,1:T(4,128)(2,1)S(1)}, bf16[2048,4]{0,1:T(4,128)(2,1)}, u32[]{:S(2)}) copy-start(bf16[2048,4]{0,1:T(4,128)(2,1)} %param.14) | copy-start | bytes 49156
  7.7 1.5 %copy-start.6 = (s32[256,2]{0,1:T(2,128)S(1)}, s32[256,2]{0,1:T(2,128)}, u32[]{:S(2)}) copy-start(s32[256,2]{0,1:T(2,128)} %param.13) | copy-start | bytes 6148
  8.8 1.3 %copy-start.2 = (bf16[256,2048]{1,0:T(8,128)(2,1)}, bf16[256,2048]{1,0:T(8,128)(2,1)S(1)}, u32[]{:S(2)}) copy-start(bf16[256,2048]{1,0:T(8,128)(2,1)S(1)} %fusion.3.normed) | copy-start | bytes 3145732

commit v2 on v1

--- a/solution.py
+++ b/solution.py
@@ -158,14 +158,15 @@
 def layer_kernel(
     experts,
     chips,
-    normed,
-    own_cols,
-    gates,
-    decoder_in,
-    queries,
-    mask,
+    source,
+    routes,
+    router_w,
+    lengths,
+    languages,
+    pivots,
     fc1_hbm,
     fc2_hbm,
+    query_hbm,
     key_hbm,
     value_hbm,
     out_hbm,
@@ -173,9 +174,13 @@
     decoded,
     fc1,
     fc2,
+    query_w,
     key_w,
     value_w,
     out_w,
+    gates,
+    decoder_in,
+    queries,
     rows,
     hidden,
     core_out,
@@ -196,7 +201,6 @@
     sum_in,
     full_in,
     load_sem,
-    own_sem,
     up_sem,
     down_sem,
     line_recv,
@@ -209,8 +213,11 @@
     end_send,
     end_recv,
 ):
-    tokens, width = normed.shape
-    columns = own_cols.shape[1]
+    tokens, width = source.shape
+    columns = encoded.shape[1]
+    parts = 2
+    part_rows = tokens // parts
+    per = columns // TILE
     e = lax.axis_index("expert")
     t = lax.axis_index("tensor")
     chip, core = t // 2, t % 2
@@ -228,7 +235,14 @@
     loads = [
         pltpu.make_async_copy(src, dst, load_sem.at[i])
         for i, (src, dst) in enumerate(
-            ((fc1_hbm, fc1), (fc2_hbm, fc2), (key_hbm, key_w), (value_hbm, value_w), (out_hbm, out_w))
+            (
+                (fc1_hbm, fc1),
+                (fc2_hbm, fc2),
+                (query_hbm, query_w),
+                (key_hbm, key_w),
+                (value_hbm, value_w),
+                (out_hbm, out_w),
+            )
         )
     ]
     for load in loads:
@@ -245,225 +259,297 @@
     def quarter(q):
         return pl.ds(pl.multiple_of(q * columns, columns), columns)
 
+    rows[e] = normalize(source[...]).astype(jnp.bfloat16)
     pl.semaphore_wait(barrier, experts + 1)
 
-    def line(b, up, from_own):
-        src = normed.at[:, quarter(t)] if from_own else rows.at[b, :, quarter(t)]
+    def line(b, up, h):
+        piece = rows.at[b, pl.ds(h * part_rows, part_rows), quarter(t)]
         return pltpu.make_async_remote_copy(
-            src_ref=src,
-            dst_ref=rows.at[b, :, quarter(t)],
-            send_sem=(up_sem if up else down_sem).at[b],
-            recv_sem=line_recv.at[b],
+            src_ref=piece,
+            dst_ref=piece,
+            send_sem=(up_sem if up else down_sem).at[b, h],
+            recv_sem=line_recv.at[b, h],
             device_id={"expert": (e + 1) % experts if up else (e + experts - 1) % experts},
             device_id_type=MESH,
         )
 
-    def spread(b, q, kind, peer):
+    def spread(b, q, h, kind, peer):
+        piece = rows.at[b, pl.ds(h * part_rows, part_rows), quarter(q)]
         return pltpu.make_async_remote_copy(
-            src_ref=rows.at[b, :, quarter(q)],
-            dst_ref=rows.at[b, :, quarter(q)],
-            send_sem=send_sem.at[kind, b],
-            recv_sem=recv_sem.at[kind, b],
+            src_ref=piece,
+            dst_ref=piece,
+            send_sem=send_sem.at[kind, b, h],
+            recv_sem=recv_sem.at[kind, b, h],
             device_id=tensor_peer[peer],
             device_id_type=MESH,
         )
 
     @pl.when(e + 1 < experts)
     def _():
-        line(e, True, True).start()
+        for h in range(parts):
+            line(e, True, h).start()
 
     @pl.when(e > 0)
     def _():
-        line(e, False, True).start()
-
-    def own_copy():
-        return pltpu.make_async_copy(normed, rows.at[e], own_sem)
-
-    own_copy().start()
-
-    def arrive(s):
+        for h in range(parts):
+            line(e, False, h).start()
+
+    def arrive(s, h):
         b = order[s]
-        line(b, True, False).wait_recv()
+        line(b, True, h).wait_recv()
 
         @pl.when((b < e) & (e + 1 < experts))
         def _():
-            line(b, True, False).start()
+            line(b, True, h).start()
 
         @pl.when((b > e) & (e > 0))
         def _():
-            line(b, False, False).start()
-
-        spread(b, t, 0, "far").start()
-        spread(b, t, 1, "mate").start()
-
-    def relay(s):
+            line(b, False, h).start()
+
+        spread(b, t, h, 0, "far").start()
+        spread(b, t, h, 1, "mate").start()
+
+    def relay(s, h):
         b = order[s]
-        spread(b, far, 0, "far").wait_recv()
-        spread(b, far, 2, "mate").start()
+        spread(b, far, h, 0, "far").wait_recv()
+        spread(b, far, h, 2, "mate").start()
 
     def ready(s):
         b = order[s]
-        spread(b, mate, 1, "mate").wait_recv()
-        spread(b, far_mate, 2, "mate").wait_recv()
-
-    def first(s):
+        for h in range(parts):
+            spread(b, mate, h, 1, "mate").wait_recv()
+            spread(b, far_mate, h, 2, "mate").wait_recv()
+
+    tiles = hidden.shape[1] // TILE
+
+    def first(s, a):
         b = order[s]
 
-        @pl.loop(0, hidden.shape[1] // TILE)
+        @pl.loop(a * (tiles // 2), (a + 1) * (tiles // 2))
         def _(j):
             at = pl.ds(pl.multiple_of(j * TILE, TILE), TILE)
             tile = jnp.dot(rows[b], fc1[:, at], preferred_element_type=jnp.float32)
             hidden[:, at] = jnp.maximum(tile, 0.0).astype(jnp.bfloat16)
 
-    per = columns // TILE
-
-    def second(s):
-        @pl.loop(0, chips * per)
-        def _(j):
-            p, k = j // per, j % per
-            start = (p * 2 + 1 - core) * columns + k * TILE
-            at = pl.ds(pl.multiple_of(start, TILE), TILE)
-            tile = jnp.dot(hidden[...], fc2[:, at], preferred_element_type=jnp.float32)
-            core_out[s, p, :, pl.ds(pl.multiple_of(k * TILE, TILE), TILE)] = tile.astype(
-                jnp.bfloat16
-            )
-
-        pair_copy(s).start()
-
-        @pl.loop(0, chips * per)
-        def _(j):
-            p, k = j // per, j % per
-            start = (p * 2 + core) * columns + k * TILE
-            at = pl.ds(pl.multiple_of(start, TILE), TILE)
-            tile = jnp.dot(hidden[...], fc2[:, at], preferred_element_type=jnp.float32)
-            kept[s, p, :, pl.ds(pl.multiple_of(k * TILE, TILE), TILE)] = tile
-
-    def pair_copy(s):
+    def second_tile(p, c, k):
+        at = pl.ds(pl.multiple_of((p * 2 + c) * columns + k * TILE, TILE), TILE)
+        return jnp.dot(hidden[...], fc2[:, at], preferred_element_type=jnp.float32)
+
+    def second(s, k):
+        @pl.loop(0, chips)
+        def _(p):
+            core_out[s, k, p] = second_tile(p, 1 - core, k).astype(jnp.bfloat16)
+
+        pair_copy(s, k).start()
+
+        @pl.loop(0, chips)
+        def _(p):
+            kept[s, k, p] = second_tile(p, core, k)
+
+    def pair_copy(s, k):
         return pltpu.make_async_remote_copy(
-            src_ref=core_out.at[s],
-            dst_ref=core_in.at[s],
-            send_sem=ret_send.at[0, s],
-            recv_sem=ret_recv.at[0, s],
+            src_ref=core_out.at[s, k],
+            dst_ref=core_in.at[s, k],
+            send_sem=ret_send.at[0, s, k],
+            recv_sem=ret_recv.at[0, s, k],
             device_id=tensor_peer["mate"],
             device_id_type=MESH,
         )
 
-    def chip_copy(s):
+    def chip_copy(s, k):
         return pltpu.make_async_remote_copy(
-            src_ref=chip_out.at[s],
-            dst_ref=chip_in.at[s],
-            send_sem=ret_send.at[1, s],
-            recv_sem=ret_recv.at[1, s],
+            src_ref=chip_out.at[s, k],
+            dst_ref=chip_in.at[s, k],
+            send_sem=ret_send.at[1, s, k],
+            recv_sem=ret_recv.at[1, s, k],
             device_id=tensor_peer["far"],
             device_id_type=MESH,
         )
 
-    def back_copy(s, b):
+    def back_copy(s, k):
         return pltpu.make_async_remote_copy(
-            src_ref=back_out.at[s],
-            dst_ref=back_in.at[e],
-            send_sem=ret_send.at[2, s],
-            recv_sem=ret_recv.at[2, e],
-            device_id={"expert": b},
+            src_ref=back_out.at[s, k],
+            dst_ref=back_in.at[e, k],
+            send_sem=ret_send.at[2, s, k],
+            recv_sem=ret_recv.at[2, e, k],
+            device_id={"expert": order[s]},
             device_id_type=MESH,
         )
 
-    def back_wait(i):
+    def back_wait(i, k):
         return pltpu.make_async_remote_copy(
-            src_ref=back_out.at[0],
-            dst_ref=back_in.at[i],
-            send_sem=ret_send.at[2, 0],
-            recv_sem=ret_recv.at[2, i],
+            src_ref=back_out.at[0, k],
+            dst_ref=back_in.at[i, k],
+            send_sem=ret_send.at[2, 0, k],
+            recv_sem=ret_recv.at[2, i, k],
             device_id={"expert": i},
             device_id_type=MESH,
         )
 
-    def reduce_pair(s):
-        pair_copy(s).wait_recv()
+    def reduce_pair(s, k):
+        pair_copy(s, k).wait_recv()
         other = 1 - chip
-        chip_out[s] = (kept[s, other] + core_in[s, other].astype(jnp.float32)).astype(jnp.bfloat16)
-        chip_copy(s).start()
-
-    def reduce_chips(s):
-        chip_copy(s).wait_recv()
+        chip_out[s, k] = (
+            kept[s, k, other] + core_in[s, k, other].astype(jnp.float32)
+        ).astype(jnp.bfloat16)
+        chip_copy(s, k).start()
+
+    def reduce_chips(s, k):
+        chip_copy(s, k).wait_recv()
         total = (
-            kept[s, chip]
-            + core_in[s, chip].astype(jnp.float32)
-            + chip_in[s].astype(jnp.float32)
+            kept[s, k, chip]
+            + core_in[s, k, chip].astype(jnp.float32)
+            + chip_in[s, k].astype(jnp.float32)
         ).astype(jnp.bfloat16)
         if s == 0:
-            back_in[e] = total
+            back_in[e, k] = total
         else:
-            back_out[s] = total
-            back_copy(s, order[s]).start()
-
-    own_copy().wait()
+            back_out[s, k] = total
+            back_copy(s, k).start()
+
+    def route():
+        logits = jnp.dot(rows[e], router_w[...], preferred_element_type=jnp.float32)
+        lane = lax.broadcasted_iota(jnp.int32, logits.shape, 1)
+        chosen = [routes[:, i : i + 1] == lane for i in range(2)]
+        picked = [jnp.sum(jnp.where(c, logits, 0.0), axis=1, keepdims=True) for c in chosen]
+        difference = picked[0] - picked[1]
+        gates[...] = jnp.where(chosen[0], jax.nn.sigmoid(difference), 0.0) + jnp.where(
+            chosen[1], jax.nn.sigmoid(-difference), 0.0
+        )
+
+    query_count, pivot_count = languages.shape
+    row_count = decoded.shape[0]
+
+    def ask():
+        place = lax.broadcasted_iota(jnp.int32, (row_count, query_count), 0)
+        query = lax.broadcasted_iota(jnp.int32, (row_count, query_count), 1)
+        below, above = query * pivot_count, (query + 1) * pivot_count
+        owner = ((place >= below) & (place < above)).astype(jnp.float32)
+        named = jnp.dot(
+            owner, languages[...].astype(jnp.float32), preferred_element_type=jnp.float32
+        )
+        first_row = jnp.zeros((row_count, pivot_count), jnp.int32)
+        place = lax.broadcasted_iota(jnp.int32, (row_count, pivot_count), 0)
+        for i in range(1, query_count):
+            first_row = first_row + jnp.where(place >= i * pivot_count, pivot_count, 0)
+        lane = lax.broadcasted_iota(jnp.int32, (row_count, pivot_count), 1)
+        language = jnp.sum(
+            jnp.where(place - first_row == lane, named, 0.0), axis=1, keepdims=True
+        )
+        pick = (jnp.abs(language - lane.astype(jnp.float32)) < 0.5).astype(jnp.bfloat16)
+        decoder_in[...] = jnp.dot(
+            pick, pivots[...], preferred_element_type=jnp.float32
+        ).astype(jnp.bfloat16)
+        loads[2].wait()
+        queries[...] = jnp.dot(
+            decoder_in[...], query_w[...], preferred_element_type=jnp.float32
+        ).astype(jnp.bfloat16)
+
     loads[0].wait()
-    first(0)
-    arrive(1)
+    first(0, 0)
+    first(0, 1)
+    arrive(1, 0)
     loads[1].wait()
-    second(0)
-    arrive(2)
-    relay(1)
-    reduce_pair(0)
+    second(0, 0)
+    arrive(1, 1)
+    second(0, 1)
+    relay(1, 0)
+    relay(1, 1)
+    arrive(2, 0)
+    route()
+    arrive(2, 1)
+    reduce_pair(0, 0)
     ready(1)
-    first(1)
-    arrive(3)
-    relay(2)
-    second(1)
-    reduce_chips(0)
-    reduce_pair(1)
-    relay(3)
+    first(1, 0)
+    arrive(3, 0)
+    relay(2, 0)
+    first(1, 1)
+    arrive(3, 1)
+    relay(2, 1)
+    reduce_pair(0, 1)
+    second(1, 0)
+    relay(3, 0)
+    second(1, 1)
+    reduce_pair(1, 0)
+    relay(3, 1)
+    reduce_chips(0, 0)
+    reduce_pair(1, 1)
     ready(2)
-    first(2)
-    second(2)
-    reduce_chips(1)
-    reduce_pair(2)
+    first(2, 0)
+    reduce_chips(0, 1)
+    first(2, 1)
+    reduce_chips(1, 0)
+    second(2, 0)
+    reduce_chips(1, 1)
+    second(2, 1)
+    reduce_pair(2, 0)
     ready(3)
-    first(3)
-    reduce_chips(2)
-    second(3)
-    reduce_pair(3)
-    reduce_chips(3)
-
-    for s in range(1, experts):
-        back_wait(order[s]).wait_recv()
-    mixed = own_cols[...].astype(jnp.float32)
-    for i in range(experts):
-        mixed = mixed + gates[:, i : i + 1] * back_in[i].astype(jnp.float32)
-    mixed = mixed.astype(jnp.bfloat16)
-    encoded[...] = mixed
-    gathered[:, quarter(t)] = mixed
-
-    def gather(q, kind, peer):
+    first(3, 0)
+    reduce_pair(2, 1)
+    first(3, 1)
+    reduce_chips(2, 0)
+    second(3, 0)
+    reduce_chips(2, 1)
+    second(3, 1)
+    reduce_pair(3, 0)
+    reduce_pair(3, 1)
+    reduce_chips(3, 0)
+    reduce_chips(3, 1)
+    ask()
+
+    def part(q, k):
+        return pl.ds(pl.multiple_of(q * columns + k * TILE, TILE), TILE)
+
+    def gather(q, k, kind, peer):
+        piece = gathered.at[:, part(q, k)]
         return pltpu.make_async_remote_copy(
-            src_ref=gathered.at[:, quarter(q)],
-            dst_ref=gathered.at[:, quarter(q)],
-            send_sem=gat_send.at[kind],
-            recv_sem=gat_recv.at[kind],
+            src_ref=piece,
+            dst_ref=piece,
+            send_sem=gat_send.at[kind, k],
+            recv_sem=gat_recv.at[kind, k],
             device_id=tensor_peer[peer],
             device_id_type=MESH,
         )
 
-    gather(t, 0, "far").start()
-    gather(t, 1, "mate").start()
-    for load in loads[2:]:
+    def project(q, k, fresh):
+        piece = gathered[:, part(q, k)]
+        for weight, total in ((key_w, key_sum), (value_w, value_sum)):
+            term = jnp.dot(piece, weight[part(q, k), :], preferred_element_type=jnp.float32)
+            total[...] = term if fresh else total[...] + term
+
+    for load in loads[3:]:
         load.wait()
-
-    def project(q, fresh):
-        part = gathered[:, quarter(q)]
-        for weight, total in ((key_w, key_sum), (value_w, value_sum)):
-            term = jnp.dot(part, weight[quarter(q), :], preferred_element_type=jnp.float32)
-            total[...] = term if fresh else total[...] + term
-
-    project(t, True)
-    gather(mate, 1, "mate").wait_recv()
-    project(mate, False)
-    gather(far, 0, "far").wait_recv()
-    gather(far, 2, "mate").start()
-    project(far, False)
-    gather(far_mate, 2, "mate").wait_recv()
-    project(far_mate, False)
+    for k in range(per):
+        for s in range(1, experts):
+            back_wait(order[s], k).wait_recv()
+        mixed = source[:, part(t, k)].astype(jnp.float32)
+        for i in range(experts):
+            mixed = mixed + gates[:, i : i + 1] * back_in[i, k].astype(jnp.float32)
+        mixed = mixed.astype(jnp.bfloat16)
+        gathered[:, part(t, k)] = mixed
+        gather(t, k, 0, "far").start()
+        gather(t, k, 1, "mate").start()
+        encoded[:, k * TILE : (k + 1) * TILE] = mixed
+        project(t, k, k == 0)
+    for k in range(per):
+        gather(mate, k, 1, "mate").wait_recv()
+        gather(far, k, 0, "far").wait_recv()
+        gather(far, k, 2, "mate").start()
+        project(mate, k, False)
+        project(far, k, False)
+    for k in range(per):
+        gather(far_mate, k, 2, "mate").wait_recv()
+        project(far_mate, k, False)
+
+    position = lax.broadcasted_iota(jnp.int32, (row_count, tokens), 1)
+    place = lax.broadcasted_iota(jnp.int32, (row_count, tokens), 0)
+    end = jnp.zeros((1, 1), jnp.int32)
+    allowed = jnp.zeros((row_count, tokens), jnp.float32)
+    for i in range(query_count):
+        begin, end = end, end + lengths[:, i : i + 1]
+        inside = (position >= begin) & (position < end)
+        inside = inside & (place >= i * pivot_count) & (place < (i + 1) * pivot_count)
+        allowed = jnp.where(inside, 1.0, allowed)
 
     for h in range(columns // HD):
         at = slice(h * HD, (h + 1) * HD)
@@ -473,7 +559,7 @@
             (((1,), (1,)), ((), ())),
             preferred_element_type=jnp.float32,
         ) * HD ** (-0.5)
-        scores = jnp.where(mask[...] > 0.5, scores, NEGATIVE)
+        scores = jnp.where(allowed > 0.5, scores, NEGATIVE)
         weights = jnp.exp(scores - jnp.max(scores, axis=1, keepdims=True))
         attention = (weights / jnp.sum(weights, axis=1, keepdims=True)).astype(jnp.bfloat16)
         context[:, at] = jnp.dot(
@@ -515,35 +601,31 @@
     total = jnp.concatenate([full_in[0], full_in[1]], axis=1).astype(jnp.float32)
     decoded[...] = normalize(decoder_in[...].astype(jnp.float32) + total).astype(jnp.bfloat16)
 
-    @pl.when(e + 1 < experts)
-    def _():
-        line(e, True, True).wait_send()
-
-    @pl.when(e > 0)
-    def _():
-        line(e, False, True).wait_send()
-
-    for s in range(experts):
-        b = order[s]
-        if s > 0:
-
-            @pl.when((b < e) & (e + 1 < experts))
+    for h in range(parts):
+        for s in range(experts):
+            b = order[s]
+
+            @pl.when((b <= e) & (e + 1 < experts))
             def _():
-                line(b, True, False).wait_send()
-
-            @pl.when((b > e) & (e > 0))
+                line(b, True, h).wait_send()
+
+            @pl.when((b >= e) & (e > 0))
             def _():
-                line(b, False, False).wait_send()
-
-            spread(b, t, 0, "far").wait_send()
-            spread(b, t, 1, "mate").wait_send()
-            spread(b, far, 2, "mate").wait_send()
-            back_copy(s, b).wait_send()
-        pair_copy(s).wait_send()
-        chip_copy(s).wait_send()
-    gather(t, 0, "far").wait_send()
-    gather(t, 1, "mate").wait_send()
-    gather(far, 2, "mate").wait_send()
+                line(b, False, h).wait_send()
+
+            if s > 0:
+                spread(b, t, h, 0, "far").wait_send()
+                spread(b, t, h, 1, "mate").wait_send()
+                spread(b, far, h, 2, "mate").wait_send()
+    for k in range(per):
+        for s in range(experts):
+            pair_copy(s, k).wait_send()
+            chip_copy(s, k).wait_send()
+            if s > 0:
+                back_copy(s, k).wait_send()
+        gather(t, k, 0, "far").wait_send()
+        gather(t, k, 1, "mate").wait_send()
+        gather(far, k, 2, "mate").wait_send()
     for end in ends:
         end.wait_send()
 
@@ -567,35 +649,9 @@
     tensor_count = lax.axis_size("tensor")
     chips = tensor_count // 2
     columns = model_width // tensor_count
-    normed = normalize(source_states).astype(jnp.bfloat16)
-    logits = jnp.dot(normed, router_weight, preferred_element_type=jnp.float32)
-    chosen = routes[:, :, None] == jnp.arange(experts, dtype=jnp.int32)[None, None, :]
-    pair_logits = jnp.sum(jnp.where(chosen, logits[:, None, :], 0.0), axis=2)
-    gate_values = jax.nn.sigmoid(pair_logits - pair_logits[:, ::-1])
-    gates = jnp.sum(jnp.where(chosen, gate_values[:, :, None], 0.0), axis=1)
-    own_cols = lax.dynamic_slice_in_dim(
-        source_states, lax.axis_index("tensor") * columns, columns, 1
-    )
-    query_count = lengths.shape[1]
-    pivot_count = pivot_states.shape[0]
-    row_count = query_count * pivot_count
-    query_iota = jnp.arange(query_count, dtype=jnp.int32)
-    query_ends = jnp.sum(
-        jnp.where(query_iota[None, :] <= query_iota[:, None], lengths[0][None, :], 0), axis=1
-    )
-    positions = jnp.arange(tok_count, dtype=jnp.int32)
-    key_owner = jnp.sum((positions[:, None] >= query_ends[None, :]).astype(jnp.int32), axis=1)
-    row_owner = jnp.arange(row_count, dtype=jnp.int32) // pivot_count
-    mask = (row_owner[:, None] == key_owner[None, :]).astype(jnp.float32)
-    language_pick = (
-        lang_ids.reshape(-1)[:, None] == jnp.arange(pivot_count, dtype=jnp.int32)[None, :]
-    ).astype(jnp.bfloat16)
-    decoder_in = jnp.dot(language_pick, pivot_states, preferred_element_type=jnp.float32).astype(
-        jnp.bfloat16
-    )
-    queries = jnp.dot(decoder_in, query_weight, preferred_element_type=jnp.float32).astype(
-        jnp.bfloat16
-    )
+    row_count = lengths.shape[1] * pivot_states.shape[0]
+    per = columns // TILE
+    parts = 2
     vmem = pl.BlockSpec(memory_space=pltpu.VMEM)
     hbm = pl.BlockSpec(memory_space=pl.ANY)
     bf16, f32, dma = jnp.bfloat16, jnp.float32, pltpu.SemaphoreType.DMA
@@ -607,23 +663,27 @@
             jax.ShapeDtypeStruct((tok_count, columns), bf16),
             jax.ShapeDtypeStruct((row_count, model_width), bf16),
         ),
-        in_specs=[vmem] * 6 + [hbm] * 5,
+        in_specs=[vmem] * 6 + [hbm] * 6,
         out_specs=(vmem, vmem),
         scratch_shapes=[
             pltpu.VMEM((model_width, units), bf16),
             pltpu.VMEM((units, model_width), bf16),
             pltpu.VMEM((model_width, columns), bf16),
             pltpu.VMEM((model_width, columns), bf16),
+            pltpu.VMEM((model_width, columns), bf16),
             pltpu.VMEM((columns, model_width), bf16),
+            pltpu.VMEM((tok_count, experts), f32),
+            pltpu.VMEM((row_count, model_width), bf16),
+            pltpu.VMEM((row_count, columns), bf16),
             pltpu.VMEM((experts, tok_count, model_width), bf16),
             pltpu.VMEM((tok_count, units), bf16),
-            pltpu.VMEM((experts, chips, tok_count, columns), bf16),
-            pltpu.VMEM((experts, chips, tok_count, columns), bf16),
-            pltpu.VMEM((experts, chips, tok_count, columns), f32),
-            pltpu.VMEM((experts, tok_count, columns), bf16),
-            pltpu.VMEM((experts, tok_count, columns), bf16),
-            pltpu.VMEM((experts, tok_count, columns), bf16),
-            pltpu.VMEM((experts, tok_count, columns), bf16),
+            pltpu.VMEM((experts, per, chips, tok_count, TILE), bf16),
+            pltpu.VMEM((experts, per, chips, tok_count, TILE), bf16),
+            pltpu.VMEM((experts, per, chips, tok_count, TILE), f32),
+            pltpu.VMEM((experts, per, tok_count, TILE), bf16),
+            pltpu.VMEM((experts, per, tok_count, TILE), bf16),
+            pltpu.VMEM((experts, per, tok_count, TILE), bf16),
+            pltpu.VMEM((experts, per, tok_count, TILE), bf16),
             pltpu.VMEM((tok_count, model_width), bf16),
             pltpu.VMEM((tok_count, columns), f32),
             pltpu.VMEM((tok_count, columns), f32),
@@ -634,17 +694,16 @@
             pltpu.VMEM((row_count, half), bf16),
             pltpu.VMEM((row_count, half), bf16),
             pltpu.VMEM((2, row_count, half), bf16),
-            dma((5,)),
-            dma,
-            dma((experts,)),
-            dma((experts,)),
-            dma((experts,)),
-            dma((3, experts)),
-            dma((3, experts)),
-            dma((3, experts)),
-            dma((3, experts)),
-            dma((3,)),
-            dma((3,)),
+            dma((6,)),
+            dma((experts, parts)),
+            dma((experts, parts)),
+            dma((experts, parts)),
+            dma((3, experts, parts)),
+            dma((3, experts, parts)),
+            dma((3, experts, per)),
+            dma((3, experts, per)),
+            dma((3, per)),
+            dma((3, per)),
             dma((3,)),
             dma((3,)),
         ],
@@ -652,14 +711,15 @@
             collective_id=0, has_side_effects=True, vmem_limit_bytes=60 * 2**20
         ),
     )(
-        normed,
-        own_cols,
-        gates,
-        decoder_in,
-        queries,
-        mask,
+        source_states,
+        routes,
+        router_weight,
+        lengths,
+        lang_ids,
+        pivot_states,
         fc1_weight[0],
         fc2_weight[0],
+        query_weight,
         key_weight,
         value_weight,
         out_weight,

time: 109 us -> 93.7 us (0.86)
  the two profiles are of different devices: /device:TPU:1 before, /device:TPU:25 now
where the time goes in v2:
time: 93.7 us; the launch traced here: 93.4 us
  Pallas kernels  86.2 us (92%)
  local copies, waits for them, and re-layouts  6.52 us (7%)
    pallas_call x1, Pallas kernels, dense_shards(): pl.pallas_call(functools.partial(layer_kernel, experts, chips), out_shape...  86.2 us
    unnamed x4, local copies, waits for them, and re-layouts  6.52 us

profile of v2, /device:TPU:25, one launch (start us, length us, event | category | flops | bytes accessed | tf_op | source)
XLA Modules:
  0.0 93.4 jit_solution(4019363375761873144)
XLA Ops:
  0.6 1.5 %copy.14.routes = s32[256,2]{1,0:T(8,128)} copy(s32[256,2]{0,1:T(2,128)} %param.13) | data formatting | bytes 4096 | tf_op args[1]
  2.1 1.8 %copy.15.router_w = bf16[2048,4]{1,0:T(8,128)(2,1)} copy(bf16[2048,4]{0,1:T(4,128)(2,1)} %param.14) | data formatting | bytes 32768 | tf_op args[2]
  3.9 86.2 %shard_map.131 = (bf16[256,512]{1,0:T(8,128)(2,1)}, bf16[48,2048]{1,0:T(8,128)(2,1)}) custom-call(bf16[256,2048]{1,0:T(8,128)(2,1)} %source.1, s32[256,2]{1,0:T(8,128)} %copy.14.routes, bf16[2048,4]{1,0:T(8,128)(2,1)} %copy.15.router_w, s32[1,8]{1,0:T(1,128)} %lengths.1, s32[8,6]{1,0:T(8,128)} %languages.1, bf16[6,2048]{1,0:T(8,128)(2,1)} %pivots.1, ...), custom_call_target="tpu_custom_call" | custom-call | tf_op jit(solution)/shard_map/pallas_call | solution.py:660
  90.1 1.7 %copy.18 = bf16[256,512]{1,0:T(8,128)(2,1)} copy(bf16[256,512]{1,0:T(8,128)(2,1)} %get-tuple-element.4) | data formatting | bytes 524288
  91.8 1.6 %copy.19 = bf16[48,2048]{1,0:T(8,128)(2,1)} copy(bf16[48,2048]{1,0:T(8,128)(2,1)} %get-tuple-element.5) | data formatting | bytes 393216

commit v3 on v2

--- a/solution.py
+++ b/solution.py
@@ -229,7 +229,10 @@
     def same(i):
         return 1 - ((e - i + experts) % experts + experts - 1) // experts
 
-    nearest = [sorted(range(experts), key=lambda b, i=i: abs(b - i)) for i in range(experts)]
+    nearest = [
+        sorted(range(experts), key=lambda b, i=i: (abs(b - i), abs(2 * b - experts + 1)))
+        for i in range(experts)
+    ]
     order = [sum(same(i) * nearest[i][s] for i in range(experts)) for s in range(experts)]
 
     loads = [
@@ -408,14 +411,20 @@
             back_copy(s, k).start()
 
     def route():
-        logits = jnp.dot(rows[e], router_w[...], preferred_element_type=jnp.float32)
-        lane = lax.broadcasted_iota(jnp.int32, logits.shape, 1)
-        chosen = [routes[:, i : i + 1] == lane for i in range(2)]
-        picked = [jnp.sum(jnp.where(c, logits, 0.0), axis=1, keepdims=True) for c in chosen]
+        logits = lax.dot_general(
+            router_w[...],
+            rows[e],
+            (((1,), (1,)), ((), ())),
+            preferred_element_type=jnp.float32,
+        )
+        place = lax.broadcasted_iota(jnp.int32, logits.shape, 0)
+        chosen = [routes[i : i + 1, :] == place for i in range(2)]
+        picked = [jnp.sum(jnp.where(c, logits, 0.0), axis=0, keepdims=True) for c in chosen]
         difference = picked[0] - picked[1]
-        gates[...] = jnp.where(chosen[0], jax.nn.sigmoid(difference), 0.0) + jnp.where(
+        table = jnp.where(chosen[0], jax.nn.sigmoid(difference), 0.0) + jnp.where(
             chosen[1], jax.nn.sigmoid(-difference), 0.0
         )
+        gates[...] = jnp.transpose(table)
 
     query_count, pivot_count = languages.shape
     row_count = decoded.shape[0]
@@ -447,18 +456,18 @@
 
     loads[0].wait()
     first(0, 0)
+    arrive(1, 0)
     first(0, 1)
-    arrive(1, 0)
+    arrive(1, 1)
     loads[1].wait()
     second(0, 0)
-    arrive(1, 1)
+    relay(1, 0)
     second(0, 1)
-    relay(1, 0)
     relay(1, 1)
     arrive(2, 0)
+    ask()
+    arrive(2, 1)
     route()
-    arrive(2, 1)
-    reduce_pair(0, 0)
     ready(1)
     first(1, 0)
     arrive(3, 0)
@@ -466,36 +475,34 @@
     first(1, 1)
     arrive(3, 1)
     relay(2, 1)
-    reduce_pair(0, 1)
     second(1, 0)
     relay(3, 0)
+    reduce_pair(1, 0)
     second(1, 1)
-    reduce_pair(1, 0)
     relay(3, 1)
-    reduce_chips(0, 0)
     reduce_pair(1, 1)
     ready(2)
     first(2, 0)
-    reduce_chips(0, 1)
     first(2, 1)
-    reduce_chips(1, 0)
     second(2, 0)
-    reduce_chips(1, 1)
+    reduce_pair(2, 0)
     second(2, 1)
-    reduce_pair(2, 0)
+    reduce_pair(2, 1)
     ready(3)
     first(3, 0)
-    reduce_pair(2, 1)
+    reduce_chips(1, 0)
     first(3, 1)
+    reduce_chips(1, 1)
+    second(3, 0)
+    reduce_pair(3, 0)
+    second(3, 1)
+    reduce_pair(3, 1)
+    reduce_pair(0, 0)
+    reduce_pair(0, 1)
     reduce_chips(2, 0)
-    second(3, 0)
     reduce_chips(2, 1)
-    second(3, 1)
-    reduce_pair(3, 0)
-    reduce_pair(3, 1)
     reduce_chips(3, 0)
     reduce_chips(3, 1)
-    ask()
 
     def part(q, k):
         return pl.ds(pl.multiple_of(q * columns + k * TILE, TILE), TILE)
@@ -520,6 +527,7 @@
     for load in loads[3:]:
         load.wait()
     for k in range(per):
+        reduce_chips(0, k)
         for s in range(1, experts):
             back_wait(order[s], k).wait_recv()
         mixed = source[:, part(t, k)].astype(jnp.float32)
@@ -712,8 +720,8 @@
         ),
     )(
         source_states,
-        routes,
-        router_weight,
+        routes.T,
+        router_weight.T,
         lengths,
         lang_ids,
         pivot_states,

time: 93.7 us -> 89.4 us (0.954)
  the two profiles are of different devices: /device:TPU:25 before, /device:TPU:1 now
where the time goes in v3:
time: 89.4 us; the launch traced here: 89.2 us
  Pallas kernels  85.2 us (95%)
  local copies, waits for them, and re-layouts  3.29 us (4%)
    pallas_call x1, Pallas kernels, dense_shards(): pl.pallas_call(functools.partial(layer_kernel, experts, chips), out_shape...  85.2 us
    unnamed x2, local copies, waits for them, and re-layouts  3.29 us

profile of v3, /device:TPU:1, one launch (start us, length us, event | category | flops | bytes accessed | tf_op | source)
XLA Modules:
  0.0 89.2 jit_solution(16048407177169689510)
XLA Ops:
  0.6 85.2 %shard_map.131 = (bf16[256,512]{1,0:T(8,128)(2,1)}, bf16[48,2048]{1,0:T(8,128)(2,1)}) custom-call(bf16[256,2048]{1,0:T(8,128)(2,1)} %source.1, s32[2,256]{1,0:T(2,128)} %bitcast.7, bf16[4,2048]{1,0:T(4,128)(2,1)} %bitcast.6, s32[1,8]{1,0:T(1,128)} %lengths.1, s32[8,6]{1,0:T(8,128)} %languages.1, bf16[6,2048]{1,0:T(8,128)(2,1)} %pivots.1, ...), custom_call_target="tpu_custom_call" | custom-call | tf_op jit(solution)/shard_map/pallas_call | solution.py:668
  85.9 1.7 %copy.16 = bf16[256,512]{1,0:T(8,128)(2,1)} copy(bf16[256,512]{1,0:T(8,128)(2,1)} %get-tuple-element.4) | data formatting | bytes 524288
  87.5 1.6 %copy.17 = bf16[48,2048]{1,0:T(8,128)(2,1)} copy(bf16[48,2048]{1,0:T(8,128)(2,1)} %get-tuple-element.5) | data formatting | bytes 393216
